TPU v7x, 512 devices: a whole 4x8x8 slice. The times are simulated.
512 devices in a mesh: grp: 32 (over y, x), mlp: 16 (over z, core).
Axes of the slice: x: 4, y: 8, z: 8, core: 2. Of those that a mesh axis runs over, the one named last changes fastest.
Arguments:
- queries: bfloat16 [32, 128, 4096], P('grp'), may hold values from -70 to 70
- fresh_kv: bfloat16 [32, 128, 1024], P('grp', 'mlp'), may hold values from -5 to 5
- kv_pages: bfloat16 [32, 32, 128, 1024], P('grp', 'mlp'), may hold values from -5 to 5
- residual: bfloat16 [32, 128, 4096], P('grp'), may hold values from -3 to 3
- norm_gain: float32 [4096], replicated, may hold values from 0.5 to 1.5
- out_weight: bfloat16 [4096, 4096], P('mlp', 'grp'), may hold values from -0.09375 to 0.09375
- gate_weight: bfloat16 [4096, 6144], P('grp', 'mlp'), may hold values from -0.09375 to 0.09375
- up_weight: bfloat16 [4096, 6144], P('grp', 'mlp'), may hold values from -0.09375 to 0.09375
- down_weight: bfloat16 [6144, 4096], P('mlp', 'grp'), may hold values from -0.078125 to 0.078125
- page_table: int32 [32, 16, 12], P('grp'), may hold values from -1 to 31, as said below
- shared_pages: int32 [32, 4], P('grp'), may hold values from 0 to 31, as said below
- cache_lens: int32 [32, 16], P('grp'), may hold values from 513 to 2048, as said below
- prefill_offsets: int32 [32], P('grp'), may hold values from 1 to 512
Outputs:
- layer_out: bfloat16 [32, 128, 4096], P('grp', 'mlp')
Inputs may be any that keep to these rules, and one draw needn't show every extreme that they name: `page_table`: row d lists the pool pages that hold decode d's tokens after the shared prompt, in order, and -1 after its last page; no page appears twice in a group, and none is also a shared page. `shared_pages`: the pool pages of the group's shared prompt in order; they are the first 4 pages of every request of the group. `cache_lens`: decode d's cached tokens fill exactly its listed pages after the 4 shared pages; in every group one decode has the most.
All inputs are finite; a program needn't handle non-finite values.
Results may differ from a plain program's by a relative error of at most 0.029.
Values may be sent and summed in bfloat16 or wider, within the bound.
No kernel may reach another device: no remote copies, remote signals or barrier semaphores. Data moves between devices by JAX's collectives and lax.ppermute only.
A program may use at most 128 MiB of HBM per device.

v0:
```python
import jax
import jax.numpy as jnp
from jax import lax
from jax.sharding import PartitionSpec as P

HEADS = 32
KV_HEADS = 4
HEAD = 128
PAGE = 128
SHARED_PAGES = 4
PRIVATE_PAGES = 12
DECODES = 16
PREFILL = 112
ROWS = 128
NEG_FILL = -1e30
EPSILON = 1e-05


def merged(shard, axis, combine):
    everything = jax.tree.map(lambda part: lax.all_gather(part, axis), shard)
    leading = jax.tree.map(lambda part: part[0], everything)

    def step(k, so_far):
        return combine(so_far, jax.tree.map(lambda part: part[k], everything))

    return lax.fori_loop(1, lax.axis_size(axis), step, leading)


def page_layout(page_ids, table_group, shared_group):
    shared_match = shared_group[None, :] == page_ids[:, None]
    is_shared = jnp.any(shared_match, axis=1)
    shared_slot = jnp.sum(
        jnp.where(shared_match, jnp.arange(SHARED_PAGES, dtype=jnp.int32)[None, :], 0),
        axis=1,
        dtype=jnp.int32,
    )
    own_match = table_group[None, :, :] == page_ids[:, None, None]
    owner_id = (
        jnp.sum(
            jnp.where(own_match, jnp.arange(DECODES, dtype=jnp.int32)[None, :, None] + 1, 0),
            axis=(1, 2),
            dtype=jnp.int32,
        )
        - 1
    )
    own_slot = jnp.sum(
        jnp.where(own_match, jnp.arange(PRIVATE_PAGES, dtype=jnp.int32)[None, None, :], 0),
        axis=(1, 2),
        dtype=jnp.int32,
    )
    page_base = jnp.where(is_shared, shared_slot * PAGE, (SHARED_PAGES + own_slot) * PAGE)
    key_pos = (page_base[:, None] + jnp.arange(PAGE, dtype=jnp.int32)[None, :]).reshape(-1)
    key_shared = jnp.repeat(is_shared, PAGE)
    key_owner = jnp.repeat(jnp.where(is_shared, -1, owner_id), PAGE)
    return (key_pos, key_shared, key_owner)


def row_layout(lens_group, offset_value):
    row_ids = jnp.arange(ROWS, dtype=jnp.int32)
    is_prefill = row_ids < PREFILL
    decode_id = jnp.where(is_prefill, -2, row_ids - PREFILL)
    picked = decode_id[:, None] == jnp.arange(DECODES, dtype=jnp.int32)[None, :]
    decode_limit = jnp.sum(jnp.where(picked, lens_group[None, :], 0), axis=1, dtype=jnp.int32)
    limit = jnp.where(is_prefill, offset_value, decode_limit)
    return (row_ids, is_prefill, decode_id, limit)


def cache_visible(key_pos, key_shared, key_owner, decode_id, limit):
    belongs = key_shared[None, :] | (key_owner[None, :] == decode_id[:, None])
    return belongs & (key_pos[None, :] < limit[:, None])


def fresh_visible(key_rows, row_ids, is_prefill):
    before = (key_rows[None, :] < PREFILL) & (key_rows[None, :] <= row_ids[:, None])
    return jnp.where(is_prefill[:, None], before, key_rows[None, :] == row_ids[:, None])


def rms_norm(values, norm_gain):
    return (
        values * lax.rsqrt(jnp.mean(values * values, axis=1, keepdims=True) + EPSILON) * norm_gain
    ).astype(jnp.bfloat16)


def combine_parts(earlier_part, later_part):
    peak_one, total_one, mixed_one = earlier_part
    peak_two, total_two, mixed_two = later_part
    row_peak = jnp.maximum(peak_one, peak_two)
    factor_one = jnp.exp(peak_one - row_peak)
    factor_two = jnp.exp(peak_two - row_peak)
    row_total = total_one * factor_one + total_two * factor_two
    row_number, head_number = row_peak.shape
    weighted = (
        mixed_one.reshape(row_number, head_number, -1) * factor_one[:, :, None]
        + mixed_two.reshape(row_number, head_number, -1) * factor_two[:, :, None]
    )
    return (row_peak, row_total, weighted.reshape(row_number, -1))


def local(
    queries,
    fresh_kv,
    kv_pages,
    residual,
    norm_gain,
    out_weight,
    gate_weight,
    up_weight,
    down_weight,
    page_table,
    shared_pages,
    cache_lens,
    prefill_offsets,
):
    out_rows, gate_cols, up_cols, down_rows = (
        lax.all_gather(out_weight, "grp", axis=1, tiled=True),
        lax.all_gather(gate_weight, "grp", axis=0, tiled=True),
        lax.all_gather(up_weight, "grp", axis=0, tiled=True),
        lax.all_gather(down_weight, "grp", axis=1, tiled=True),
    )
    mlp_index = lax.axis_index("mlp")
    pool_pages = kv_pages.shape[1]
    own_count = fresh_kv.shape[1]
    page_ids = mlp_index * pool_pages + jnp.arange(pool_pages, dtype=jnp.int32)
    key_rows = mlp_index * own_count + jnp.arange(own_count, dtype=jnp.int32)
    key_pos, key_shared, key_owner = page_layout(page_ids, page_table[0], shared_pages[0])
    row_ids, is_prefill, decode_id, limit = row_layout(cache_lens[0], prefill_offsets[0])
    cache_seen = cache_visible(key_pos, key_shared, key_owner, decode_id, limit)
    fresh_seen = fresh_visible(key_rows, row_ids, is_prefill)
    cached = kv_pages[0].reshape(pool_pages * PAGE, 2, KV_HEADS, HEAD)
    fresh = fresh_kv[0].reshape(own_count, 2, KV_HEADS, HEAD)
    grouped = HEADS // KV_HEADS
    query_heads = queries[0].reshape(ROWS, KV_HEADS, grouped, HEAD)
    score_scale = HEAD ** (-0.5)
    peak_list = []
    total_list = []
    mixed_list = []
    for head_index in range(KV_HEADS):
        query_block = query_heads[:, head_index]
        cache_scores = (
            jnp.einsum(
                "rgh,kh->rgk",
                query_block,
                cached[:, 0, head_index],
                preferred_element_type=jnp.float32,
            )
            * score_scale
        )
        fresh_scores = (
            jnp.einsum(
                "rgh,kh->rgk",
                query_block,
                fresh[:, 0, head_index],
                preferred_element_type=jnp.float32,
            )
            * score_scale
        )
        cache_scores = jnp.where(cache_seen[:, None, :], cache_scores, NEG_FILL)
        fresh_scores = jnp.where(fresh_seen[:, None, :], fresh_scores, NEG_FILL)
        row_peak = jnp.maximum(jnp.max(cache_scores, axis=2), jnp.max(fresh_scores, axis=2))
        cache_exps = jnp.where(
            cache_seen[:, None, :], jnp.exp(cache_scores - row_peak[:, :, None]), 0.0
        )
        fresh_exps = jnp.where(
            fresh_seen[:, None, :], jnp.exp(fresh_scores - row_peak[:, :, None]), 0.0
        )
        row_total = jnp.sum(cache_exps, axis=2) + jnp.sum(fresh_exps, axis=2)
        weighted = jnp.einsum(
            "rgk,kh->rgh",
            cache_exps.astype(jnp.bfloat16),
            cached[:, 1, head_index],
            preferred_element_type=jnp.float32,
        )
        weighted = weighted + jnp.einsum(
            "rgk,kh->rgh",
            fresh_exps.astype(jnp.bfloat16),
            fresh[:, 1, head_index],
            preferred_element_type=jnp.float32,
        )
        peak_list.append(row_peak)
        total_list.append(row_total)
        mixed_list.append(weighted)
    row_peak = jnp.stack(peak_list, axis=1).reshape(ROWS, HEADS)
    row_total = jnp.stack(total_list, axis=1).reshape(ROWS, HEADS)
    weighted = jnp.stack(mixed_list, axis=1).reshape(ROWS, HEADS * HEAD)
    row_peak, row_total, weighted = merged((row_peak, row_total, weighted), "mlp", combine_parts)
    attended = (
        (weighted.reshape(ROWS, HEADS, HEAD) / row_total[:, :, None])
        .reshape(ROWS, HEADS * HEAD)
        .astype(jnp.bfloat16)
    )
    feature_count = out_rows.shape[0]
    own_features = lax.dynamic_slice_in_dim(attended, mlp_index * feature_count, feature_count, 1)
    row_begin = mlp_index * own_count
    projected = lax.psum(
        jnp.dot(own_features, out_rows, preferred_element_type=jnp.float32).astype(jnp.bfloat16),
        "mlp",
    ).astype(jnp.float32)
    updated = residual[0].astype(jnp.float32) + projected
    normed = rms_norm(updated, norm_gain)
    carried_rows = lax.dynamic_slice_in_dim(updated, row_begin, own_count, 0)
    gate_act = jnp.dot(normed, gate_cols, preferred_element_type=jnp.float32)
    up_act = jnp.dot(normed, up_cols, preferred_element_type=jnp.float32)
    hidden = (jax.nn.silu(gate_act) * up_act).astype(jnp.bfloat16)
    returned = lax.psum_scatter(
        jnp.dot(hidden, down_rows, preferred_element_type=jnp.float32).astype(jnp.bfloat16),
        "mlp",
        scatter_dimension=0,
        tiled=True,
    ).astype(jnp.float32)
    return (carried_rows + returned).astype(jnp.bfloat16)[None]


def solution(mesh):
    placed = (
        P("grp", None, None),
        P("grp", "mlp", None),
        P("grp", "mlp", None, None),
        P("grp", None, None),
        P(),
        P("mlp", "grp"),
        P("grp", "mlp"),
        P("grp", "mlp"),
        P("mlp", "grp"),
        P("grp", None, None),
        P("grp", None),
        P("grp", None),
        P("grp"),
    )
    return jax.shard_map(
        local, mesh=mesh, in_specs=placed, out_specs=P("grp", "mlp", None), check_vma=False
    )
```

profile of v0, /device:TPU:2, one launch (start us, length us, event | category | flops | bytes accessed | tf_op | source)
XLA Modules:
  0.0 786.7 jit_solution(5587190281900795073)
XLA Ops:
  6.6 0.9 compare_reduce_fusion
  7.5 0.8 fusion.85
  8.3 1.6 copy.59
  10.1 0.8 fusion.107
  14.3 1.6 fusion.99
  16.5 1.0 fusion.106
  17.5 1.9 fusion.104
  19.4 1.8 copy.89
  21.2 2.0 fusion.102
  23.2 0.9 copy.90
  24.1 2.9 fusion.100
  28.3 1.0 fusion.10
  29.7 1.0 fusion.9
  31.2 0.9 fusion.8
  32.6 0.9 fusion.7
  33.8 1.8 copy.72
  37.2 2.4 fusion.17
  39.7 24.5 %all_gather.22 = f32[16,128,32]{1,2,0:T(8,128)S(1)} all-gather(f32[1,128,32]{1,2,0:T(8,128)S(1)} %maximum_bitcast_fusion.1), channel_id=1, replica_groups=mesh['grp'=32,'mlp'=16] {'mlp'}, dimensions={0}, use_global_device_ids=true | all-gather | bytes 278528 | tf_op jit(solution)/shard_map/all_gather | solution.py:20
  64.3 16.6 %all_gather.21 = f32[16,128,32]{1,2,0:T(8,128)S(1)} all-gather(f32[1,128,32]{1,2,0:T(8,128)S(1)} %maximum_bitcast_fusion), channel_id=1, replica_groups=mesh['grp'=32,'mlp'=16] {'mlp'}, dimensions={0}, use_global_device_ids=true | all-gather | bytes 278528 | tf_op jit(solution)/shard_map/all_gather | solution.py:20
  81.0 139.0 %all-gather.6.cloned.1.call-done = f32[16,128,4096]{2,1,0:T(8,128)} async-done(((f32[1,128,4096]{2,1,0:T(8,128)}), f32[16,128,4096]{2,1,0:T(8,128)}) %all-gather.6.cloned.1.call-update) | async-done | bytes 33554448 | tf_op jit(solution)/shard_map/all_gather | solution.py:20
  220.0 1.7 slice_bitcast_fusion
  221.8 108.8 %while.19 = (s32[]{:T(128)}, f32[128,32]{1,0:T(8,128)S(1)}, f32[128,32]{1,0:T(8,128)S(1)}, f32[128,4096]{1,0:T(8,128)S(1)}, f32[16,128,32]{1,2,0:T(8,128)S(1)}, ...) while((s32[]{:T(128)}, f32[128,32]{1,0:T(8,128)S(1)}, ...), condition=%wide.region_22.23_spmd, body=%wide.region_21.22_spmd.sunk | while | flops 1597445 | bytes 14975127 | solution.py:26
  223.3 5.7 fusion.115
  230.6 5.7 fusion.115
  237.8 5.7 fusion.115
  245.1 5.7 fusion.115
  252.3 5.7 fusion.115
  259.6 5.7 fusion.115
  266.8 5.7 fusion.115
  274.1 5.7 fusion.115
  281.3 5.7 fusion.115
  288.6 5.7 fusion.115
  295.9 5.7 fusion.115
  303.1 5.7 fusion.115
  310.4 5.7 fusion.115
  317.6 5.7 fusion.115
  324.9 5.7 fusion.115
  331.2 3.0 copy.115
  334.2 3.2 convolution_convert_fusion.1
  339.2 114.0 %all-reduce.2.cloned.1.call-done = bf16[128,4096]{1,0:T(8,128)(2,1)} async-done(((bf16[128,4096]{1,0:T(8,128)(2,1)}), bf16[128,4096]{1,0:T(8,128)(2,1)}) %all-reduce.2.cloned.1.call-update) | async-done | bytes 1048592 | tf_op jit(solution)/shard_map/psum | solution.py:194
  453.3 3.0 convert_add_fusion
  456.2 84.0 %all-gather.10.cloned.1.call-done = bf16[4096,384]{1,0:T(8,128)(2,1)} async-done(((bf16[128,384]{1,0:T(8,128)(2,1)}), bf16[4096,384]{1,0:T(8,128)(2,1)}) %all-gather.10.cloned.1.call-update) | async-done | bytes 3145744 | tf_op jit(solution)/shard_map/all_gather | solution.py:116
  540.3 2.6 fusion.97
  542.9 83.0 %all-gather.12.cloned.1.call-done = bf16[4096,384]{1,0:T(8,128)(2,1)} async-done(((bf16[128,384]{1,0:T(8,128)(2,1)}), bf16[4096,384]{1,0:T(8,128)(2,1)}) %all-gather.12.cloned.1.call-update) | async-done | bytes 3145744 | tf_op jit(solution)/shard_map/all_gather | solution.py:117
  625.9 86.5 %all-gather.14.cloned.1.call-done = bf16[384,4096]{1,0:T(8,128)(2,1)} async-done(((bf16[384,128]{1,0:T(8,128)(2,1)}), bf16[384,4096]{1,0:T(8,128)(2,1)}) %all-gather.14.cloned.1.call-update) | async-done | bytes 3145744 | tf_op jit(solution)/shard_map/all_gather | solution.py:118
  712.5 5.3 convolution_convert_fusion
  717.8 60.5 %reduce-scatter.2.cloned.1.call-done = bf16[8,4096]{1,0:T(8,128)(2,1)} async-done(((bf16[128,4096]{1,0:T(8,128)(2,1)}), bf16[8,4096]{1,0:T(8,128)(2,1)}) %reduce-scatter.2.cloned.1.call-update) | async-done | bytes 65552 | tf_op jit(solution)/shard_map/reduce_scatter | solution.py:204
  778.2 1.6 fusion.51
  (190 shorter events, 32.3 us)
Async XLA Ops:
  6.5 3.5 copy-start.16
  6.5 6.6 copy-start.15
  6.5 7.4 copy-start.8
  6.5 213.5 %all-gather.6.cloned.1.call-start = ((), (), s32[]{:S(2)}) async-start(), calls=%async_computation.1 | async-start | bytes 35651584 | tf_op jit(solution)/shard_map/all_gather | solution.py:20
  10.0 7.5 copy-start.7
  11.7 4.6 copy-start.20
  19.4 9.8 %copy-start.2 = (f32[128,8,256]{2,0,1:T(8,128)}, f32[128,8,256]{2,0,1:T(8,128)S(1)}, u32[]{:S(2)}) copy-start(f32[128,8,256]{2,0,1:T(8,128)S(1)} %get-tuple-element.256) | copy-start | bytes 3145732
  23.2 7.6 copy-start.4
  24.1 5.2 copy-start.10
  27.1 2.1 copy-start.19
  27.8 1.9 copy-start.11
  28.2 2.5 copy-start.18
  28.2 2.6 copy-start.9
  29.3 1.9 copy-start.12
  29.7 2.5 copy-start.17
  29.7 2.5 copy-start.6
  30.8 1.8 copy-start.13
  35.6 1.2 copy-start.3
  35.6 1.5 copy-start.5
  35.7 298.6 %all-gather.8.cloned.1.call-start = ((), (), s32[]{:S(2)}) async-start(), calls=%async_computation.2 | async-start | bytes 2162688 | tf_op jit(solution)/shard_map/all_gather | solution.py:115
  36.4 416.8 %all-reduce.2.cloned.1.call-start = ((), (), s32[]{:S(2)}) async-start(), calls=%async_computation.3 | async-start | bytes 2097152 | tf_op jit(solution)/shard_map/psum | solution.py:194
  334.2 119.0 %copy-start = (bf16[1,128,4096]{2,1,0:T(8,128)(2,1)S(1)}, bf16[1,128,4096]{2,1,0:T(8,128)(2,1)}, u32[]{:S(2)}) copy-start(bf16[1,128,4096]{2,1,0:T(8,128)(2,1)} %param.18) | copy-start | bytes 3145732
  337.4 202.8 %all-gather.10.cloned.1.call-start = ((), (), s32[]{:S(2)}) async-start(), calls=%async_computation.4 | async-start | bytes 3244032 | tf_op jit(solution)/shard_map/all_gather | solution.py:116
  338.0 287.9 %all-gather.12.cloned.1.call-start = ((), (), s32[]{:S(2)}) async-start(), calls=%async_computation.5 | async-start | bytes 3244032 | tf_op jit(solution)/shard_map/all_gather | solution.py:117
  338.6 373.9 %all-gather.14.cloned.1.call-start = ((), (), s32[]{:S(2)}) async-start(), calls=%async_computation.6 | async-start | bytes 3244032 | tf_op jit(solution)/shard_map/all_gather | solution.py:118
  339.2 201.1 %copy-start.14 = (f32[4096]{0:T(1024)S(1)}, f32[4096]{0:T(1024)}, u32[]{:S(2)}) copy-start(f32[4096]{0:T(1024)} %param.19) | copy-start | bytes 49156
  339.2 439.1 %reduce-scatter.2.cloned.1.call-start = ((), (), s32[]{:S(2)}) async-start(), calls=%async_computation.7 | async-start | bytes 1114112 | tf_op jit(solution)/shard_map/reduce_scatter | solution.py:204
  453.2 87.0 %copy-start.1 = (bf16[128,4096]{1,0:T(8,128)(2,1)S(1)}, bf16[128,4096]{1,0:T(8,128)(2,1)}, u32[]{:S(2)}) copy-start(bf16[128,4096]{1,0:T(8,128)(2,1)} %all-reduce.2.cloned.1.call-done) | copy-start | bytes 3145732
Sparse Core Ops, SparseCore 0:
  35.8 184.2 all-gather.5
  223.1 77.9 all-gather.7
  337.5 115.6 all-reduce.1
  456.7 83.4 all-gather.9
  543.8 82.1 all-gather.11
  629.3 83.1 all-gather.13
  717.9 60.2 reduce-scatter.1
where the time goes:
time: 788 us; the launch traced here: 787 us
  waiting for transfers between devices  569 us (72%)
  other arithmetic  97.4 us (12%)
  blocking collectives  41.1 us (5%)
  local copies, waits for them, and re-layouts  35.7 us (5%)
  matrix products  27.6 us (4%)
  between operations  14.6 us (2%)
    all_gather x1, waiting for transfers between devices, merged(): everything = jax.tree.map(lambda part: lax.all_gather(part, axis), shard)  139 us
    psum x1, waiting for transfers between devices, local(): lax.psum(jnp.dot(own_features, out_rows, preferred_element_type=jnp.float...  114 us
    all_gather x1, waiting for transfers between devices, local(): lax.all_gather(down_weight, 'grp', axis=1, tiled=True)  86.5 us
    add x15, other arithmetic, combine_parts(): mixed_one.reshape(row_number, head_number, -1) * factor_one[:, :, None]  86.1 us
    all_gather x1, waiting for transfers between devices, local(): lax.all_gather(gate_weight, 'grp', axis=0, tiled=True)  84 us
    all_gather x1, waiting for transfers between devices, local(): lax.all_gather(up_weight, 'grp', axis=0, tiled=True)  83 us
    reduce_scatter x1, waiting for transfers between devices, local(): lax.psum_scatter(jnp.dot(hidden, down_rows, preferred_element_type=jnp.fl...  60.5 us
    all_gather x2, blocking collectives, merged(): everything = jax.tree.map(lambda part: lax.all_gather(part, axis), shard)  41.1 us
  transfers between devices with their start and end apart: 7, of which 6 were waited for; matrix products, arithmetic and copies ran while one was open for 15% of the time, Pallas kernels for 0%

commit v1 on v0

--- a/solution.py
+++ b/solution.py
@@ -14,6 +14,14 @@
 ROWS = 128
 NEG_FILL = -1e30
 EPSILON = 1e-05
+
+
+def gather_by_exchange(shard, axis, dim):
+    length = lax.axis_size(axis)
+    repeats = [length if d == dim else 1 for d in range(shard.ndim)]
+    return lax.all_to_all(
+        jnp.tile(shard, repeats), axis, split_axis=dim, concat_axis=dim, tiled=True
+    )
 
 
 def merged(shard, axis, combine):
@@ -115,7 +123,7 @@
         lax.all_gather(out_weight, "grp", axis=1, tiled=True),
         lax.all_gather(gate_weight, "grp", axis=0, tiled=True),
         lax.all_gather(up_weight, "grp", axis=0, tiled=True),
-        lax.all_gather(down_weight, "grp", axis=1, tiled=True),
+        gather_by_exchange(down_weight, "grp", 1),
     )
     mlp_index = lax.axis_index("mlp")
     pool_pages = kv_pages.shape[1]

time: 788 us -> 702 us (0.89)
  waiting for transfers between devices: 569 us -> 467 us
  starting transfers between devices: 0.24 us -> 10.3 us
    all_gather x1 -> x0, waiting for transfers between devices: 86.5 us -> none  [local(): lax.all_gather(down_weight, 'grp', axis=1, tiled=True)]
    psum x1, waiting for transfers between devices: 114 us -> 29.6 us  [local(): lax.psum(jnp.dot(own_features, out_rows, preferred_element_type=jnp.float...]
    all_to_all x0 -> x1, waiting for transfers between devices: none -> 71.1 us  [gather_by_exchange(): lax.all_to_all(jnp.tile(shard, repeats), axis, split_axis=dim, concat_axi...]
    all_to_all x0 -> x1, starting transfers between devices: none -> 9.88 us  [gather_by_exchange(): lax.all_to_all(jnp.tile(shard, repeats), axis, split_axis=dim, concat_axi...]
  transfers between devices with their start and end apart: 7 -> 7, of which waited for: 6 -> 6; matrix products, arithmetic and copies ran while one was open for 15% -> 18% of each run, Pallas kernels for 0% -> 0%
where the time goes in v1:
time: 702 us; the launch traced here: 700 us
  waiting for transfers between devices  467 us (67%)
  other arithmetic  97.6 us (14%)
  blocking collectives  41.2 us (6%)
  local copies, waits for them, and re-layouts  41 us (6%)
  matrix products  28.2 us (4%)
  between operations  14.6 us (2%)
  starting transfers between devices  10.3 us (1%)
    all_gather x1, waiting for transfers between devices, merged(): everything = jax.tree.map(lambda part: lax.all_gather(part, axis), shard)  139 us
    add x15, other arithmetic, combine_parts(): mixed_one.reshape(row_number, head_number, -1) * factor_one[:, :, None]  86.1 us
    all_gather x1, waiting for transfers between devices, local(): lax.all_gather(gate_weight, 'grp', axis=0, tiled=True)  83.9 us
    all_gather x1, waiting for transfers between devices, local(): lax.all_gather(up_weight, 'grp', axis=0, tiled=True)  82.4 us
    all_to_all x1, waiting for transfers between devices, gather_by_exchange(): lax.all_to_all(jnp.tile(shard, repeats), axis, split_axis=dim, concat_axi...  71.1 us
    reduce_scatter x1, waiting for transfers between devices, local(): lax.psum_scatter(jnp.dot(hidden, down_rows, preferred_element_type=jnp.fl...  59.2 us
    all_gather x2, blocking collectives, merged(): everything = jax.tree.map(lambda part: lax.all_gather(part, axis), shard)  41.2 us
    psum x1, waiting for transfers between devices, local(): lax.psum(jnp.dot(own_features, out_rows, preferred_element_type=jnp.float...  29.6 us
  transfers between devices with their start and end apart: 7, of which 6 were waited for; matrix products, arithmetic and copies ran while one was open for 18% of the time, Pallas kernels for 0%

profile of v1, /device:TPU:2, one launch (start us, length us, event | category | flops | bytes accessed | tf_op | source)
XLA Modules:
  0.0 700.4 jit_solution(10766384011892757958)
XLA Ops:
  6.6 0.9 compare_reduce_fusion
  8.3 1.6 copy.79
  14.3 1.6 fusion.99
  16.5 1.0 fusion.106
  17.5 1.9 fusion.104
  19.4 1.8 copy.110
  21.2 2.0 fusion.102
  24.1 2.9 fusion.100
  28.3 1.0 fusion.10
  29.7 1.0 fusion.9
  31.2 0.9 fusion.8
  32.6 0.9 fusion.7
  33.8 1.8 copy.92
  37.2 2.4 fusion.17
  39.7 24.5 %all_gather.19 = f32[16,128,32]{1,2,0:T(8,128)S(1)} all-gather(f32[1,128,32]{1,2,0:T(8,128)S(1)} %maximum_bitcast_fusion.1), channel_id=1, replica_groups=mesh['grp'=32,'mlp'=16] {'mlp'}, dimensions={0}, use_global_device_ids=true | all-gather | bytes 278528 | tf_op jit(solution)/shard_map/all_gather | solution.py:28
  64.3 16.6 %all_gather.18 = f32[16,128,32]{1,2,0:T(8,128)S(1)} all-gather(f32[1,128,32]{1,2,0:T(8,128)S(1)} %maximum_bitcast_fusion), channel_id=1, replica_groups=mesh['grp'=32,'mlp'=16] {'mlp'}, dimensions={0}, use_global_device_ids=true | all-gather | bytes 278528 | tf_op jit(solution)/shard_map/all_gather | solution.py:28
  81.0 139.0 %all-gather.5.cloned.1.call-done = f32[16,128,4096]{2,1,0:T(8,128)} async-done(((f32[1,128,4096]{2,1,0:T(8,128)}), f32[16,128,4096]{2,1,0:T(8,128)}) %all-gather.5.cloned.1.call-update) | async-done | bytes 33554448 | tf_op jit(solution)/shard_map/all_gather | solution.py:28
  220.0 1.7 slice_bitcast_fusion
  221.8 108.8 %while.19 = (s32[]{:T(128)}, f32[128,32]{1,0:T(8,128)S(1)}, f32[128,32]{1,0:T(8,128)S(1)}, f32[128,4096]{1,0:T(8,128)S(1)}, f32[16,128,32]{1,2,0:T(8,128)S(1)}, ...) while((s32[]{:T(128)}, f32[128,32]{1,0:T(8,128)S(1)}, ...), condition=%wide.region_22.23_spmd, body=%wide.region_21.22_spmd.sunk | while | flops 1597445 | bytes 14975127 | solution.py:34
  223.3 5.7 fusion.115
  230.6 5.7 fusion.115
  237.8 5.7 fusion.115
  245.1 5.7 fusion.115
  252.3 5.7 fusion.115
  259.6 5.7 fusion.115
  266.8 5.7 fusion.115
  274.1 5.7 fusion.115
  281.3 5.7 fusion.115
  288.6 5.7 fusion.115
  295.9 5.7 fusion.115
  303.1 5.7 fusion.115
  310.4 5.7 fusion.115
  317.6 5.7 fusion.115
  324.9 5.7 fusion.115
  331.2 3.0 copy.136
  334.2 3.1 convolution_convert_fusion.1
  338.0 2.4 tile.2
  340.4 9.9 %all-to-all-start = ((bf16[384,32,128]{2,0,1:T(8,128)(2,1)}), bf16[384,32,128]{2,0,1:T(8,128)(2,1)S(1)}, u32[]{:S(2)}, u32[]{:S(2)}) async-start(bf16[384,32,128]{2,0,1:T(8,128)(2,1)} %tile.2), calls=%async_computation | async-start | bytes 6291456 | tf_op jit(solution)/shard_map/all_to_all | solution.py:22
  351.1 71.1 %all-to-all-done = bf16[384,32,128]{2,0,1:T(8,128)(2,1)S(1)} async-done(((bf16[384,32,128]{2,0,1:T(8,128)(2,1)}), bf16[384,32,128]{2,0,1:T(8,128)(2,1)S(1)}, u32[]{:S(2)}, u32[]{:S(2)}) %all-to-all-start) | async-done | bytes 3145760 | tf_op jit(solution)/shard_map/all_to_all | solution.py:22
  422.3 2.9 copy.97
  425.1 29.6 %all-reduce.2.cloned.1.call-done = bf16[128,4096]{1,0:T(8,128)(2,1)} async-done(((bf16[128,4096]{1,0:T(8,128)(2,1)}), bf16[128,4096]{1,0:T(8,128)(2,1)}) %all-reduce.2.cloned.1.call-update) | async-done | bytes 1048592 | tf_op jit(solution)/shard_map/psum | solution.py:202
  454.7 3.2 convert_add_fusion
  458.0 83.9 %all-gather.9.cloned.1.call-done = bf16[4096,384]{1,0:T(8,128)(2,1)} async-done(((bf16[128,384]{1,0:T(8,128)(2,1)}), bf16[4096,384]{1,0:T(8,128)(2,1)}) %all-gather.9.cloned.1.call-update) | async-done | bytes 3145744 | tf_op jit(solution)/shard_map/all_gather | solution.py:124
  541.8 3.3 fusion.97
  545.1 82.4 %all-gather.11.cloned.1.call-done = bf16[4096,384]{1,0:T(8,128)(2,1)} async-done(((bf16[128,384]{1,0:T(8,128)(2,1)}), bf16[4096,384]{1,0:T(8,128)(2,1)}) %all-gather.11.cloned.1.call-update) | async-done | bytes 3145744 | tf_op jit(solution)/shard_map/all_gather | solution.py:125
  627.5 5.3 convolution_convert_fusion
  632.8 59.2 %reduce-scatter.2.cloned.1.call-done = bf16[8,4096]{1,0:T(8,128)(2,1)} async-done(((bf16[128,4096]{1,0:T(8,128)(2,1)}), bf16[8,4096]{1,0:T(8,128)(2,1)}) %reduce-scatter.2.cloned.1.call-update) | async-done | bytes 65552 | tf_op jit(solution)/shard_map/reduce_scatter | solution.py:212
  692.0 1.6 fusion.51
  (191 shorter events, 34.6 us)
Async XLA Ops:
  6.5 3.5 copy-start.16
  6.5 6.6 copy-start.15
  6.5 7.4 %copy-start.7 = (bf16[1,2,128,1024]{3,2,1,0:T(8,128)(2,1)S(1)}, bf16[1,2,128,1024]{3,2,1,0:T(8,128)(2,1)}, u32[]{:S(2)}) copy-start(bf16[1,2,128,1024]{3,2,1,0:T(8,128)(2,1)} %param.17) | copy-start | bytes 1572868
  6.5 213.5 %all-gather.5.cloned.1.call-start = ((), (), s32[]{:S(2)}) async-start(), calls=%async_computation.2 | async-start | bytes 35651584 | tf_op jit(solution)/shard_map/all_gather | solution.py:28
  10.0 7.5 %copy-start.6 = (bf16[1,128,4096]{1,2,0:T(8,128)(2,1)}, bf16[1,128,4096]{1,2,0:T(8,128)(2,1)S(1)}, u32[]{:S(2)}) copy-start(bf16[1,128,4096]{1,2,0:T(8,128)(2,1)S(1)} %copy.79) | copy-start | bytes 3145732
  11.7 4.6 copy-start.20
  19.4 9.8 %copy-start.1 = (f32[128,8,256]{2,0,1:T(8,128)}, f32[128,8,256]{2,0,1:T(8,128)S(1)}, u32[]{:S(2)}) copy-start(f32[128,8,256]{2,0,1:T(8,128)S(1)} %get-tuple-element.263) | copy-start | bytes 3145732
  23.2 7.6 %copy-start.3 = (f32[128,8,256]{2,0,1:T(8,128)}, f32[128,8,256]{2,0,1:T(8,128)S(1)}, u32[]{:S(2)}) copy-start(f32[128,8,256]{2,0,1:T(8,128)S(1)} %get-tuple-element.259) | copy-start | bytes 3145732
  24.1 5.2 copy-start.9
  27.1 2.1 copy-start.19
  27.8 1.9 copy-start.10
  28.2 2.5 copy-start.18
  28.2 2.6 copy-start.8
  29.3 1.9 copy-start.11
  29.7 2.5 copy-start.17
  29.7 2.5 copy-start.5
  30.8 1.8 copy-start.12
  35.6 1.2 copy-start.2
  35.6 1.5 copy-start.4
  35.7 298.6 %all-gather.7.cloned.1.call-start = ((), (), s32[]{:S(2)}) async-start(), calls=%async_computation.3 | async-start | bytes 2162688 | tf_op jit(solution)/shard_map/all_gather | solution.py:123
  36.4 418.3 %all-reduce.2.cloned.1.call-start = ((), (), s32[]{:S(2)}) async-start(), calls=%async_computation.4 | async-start | bytes 2097152 | tf_op jit(solution)/shard_map/psum | solution.py:202
  334.2 3.7 copy-start.13
  337.4 204.4 %all-gather.9.cloned.1.call-start = ((), (), s32[]{:S(2)}) async-start(), calls=%async_computation.5 | async-start | bytes 3244032 | tf_op jit(solution)/shard_map/all_gather | solution.py:124
  340.4 81.9 %all-to-all-start = ((bf16[384,32,128]{2,0,1:T(8,128)(2,1)}), bf16[384,32,128]{2,0,1:T(8,128)(2,1)S(1)}, u32[]{:S(2)}, u32[]{:S(2)}) async-start(bf16[384,32,128]{2,0,1:T(8,128)(2,1)} %tile.2), calls=%async_computation | async-start | bytes 6291456 | tf_op jit(solution)/shard_map/all_to_all | solution.py:22
  350.3 277.2 %all-gather.11.cloned.1.call-start = ((), (), s32[]{:S(2)}) async-start(), calls=%async_computation.6 | async-start | bytes 3244032 | tf_op jit(solution)/shard_map/all_gather | solution.py:125
  350.9 341.2 %reduce-scatter.2.cloned.1.call-start = ((), (), s32[]{:S(2)}) async-start(), calls=%async_computation.7 | async-start | bytes 1114112 | tf_op jit(solution)/shard_map/reduce_scatter | solution.py:212
  425.1 116.7 %copy-start.14 = (f32[4096]{0:T(1024)S(1)}, f32[4096]{0:T(1024)}, u32[]{:S(2)}) copy-start(f32[4096]{0:T(1024)} %param.19) | copy-start | bytes 49156
  458.0 169.5 %copy-start = (bf16[384,32,128]{0,2,1:T(8,128)(2,1)S(1)}, bf16[384,32,128]{0,2,1:T(8,128)(2,1)}, u32[]{:S(2)}) copy-start(bf16[384,32,128]{0,2,1:T(8,128)(2,1)} %copy.97) | copy-start | bytes 9437188
Sparse Core Ops, SparseCore 0:
  35.8 184.2 all-gather.4
  223.1 77.9 all-gather.6
  337.5 117.1 all-reduce.1
  458.2 83.5 all-gather.8
  545.3 82.1 all-gather.10
  632.9 59.0 reduce-scatter.1
